TPU v7x, 32 devices: a whole 2x2x4 slice. The times are simulated.
32 devices in a mesh: lat: 4 (over y, core), lon: 8 (over z, x).
Axes of the slice: x: 2, y: 2, z: 4, core: 2. Of those that a mesh axis runs over, the one named last changes fastest.
Arguments:
- transport: float32 [4, 36, 128, 1024], P(None, None, 'lat', 'lon'), may hold values from 0.03 to 0.24
- mixing: float32 [35, 128, 1024], P(None, 'lat', 'lon'), may hold values from 0.05 to 5
- trajectory: bfloat16 [4, 3, 36, 128, 1024], P(None, None, None, 'lat', 'lon'), may hold values from -6 to 6
- kernel_table: float32 [64, 36], replicated, may hold values from 0 to 0.5
- track_tile: int32 [4, 16384, 1], P(None, ('lat', 'lon')), may hold values from 0 to 31; in each aligned block of 512 rows (0 to 511, 512 to 1023, ..., all dimensions but the last counted through in order) at most 32 rows name the same one
- sound_cell: int32 [4, 16384], P(None, ('lat', 'lon')), may hold values from 0 to 4095
- kernel_index: int32 [4, 16384], P(None, ('lat', 'lon')), may hold values from 0 to 63
- observed: float32 [4, 3, 16384], P(None, None, ('lat', 'lon')), may hold values from -8 to 8
- precision: float32 [4, 16384], P(None, ('lat', 'lon')), may hold values from 0.3 to 3
Outputs:
- adjoint_field: float32 [3, 36, 128, 1024], P(None, None, 'lat', 'lon')
- flux_grad: float32 [3, 128, 1024], P(None, 'lat', 'lon')
Inputs may be any that keep to these rules, and one draw needn't show every extreme that they name: `track_tile`: within one step, the soundings held by one device name any one tile at most 32 times, and some device names some tile exactly 32 times.
All inputs are finite; a program needn't handle non-finite values.
Results may differ from a plain program's by a relative error of at most 0.0003.
Values may be sent and summed in bfloat16 or wider, within the bound.
A program may use at most 128 MiB of HBM per device.

v0:
```python
import functools

import jax
import jax.numpy as jnp
from jax import lax
from jax.experimental import pallas as pl
from jax.experimental.pallas import tpu as pltpu
from jax.sharding import PartitionSpec as P

F32 = jnp.float32
BF16 = jnp.bfloat16
MESH = pl.DeviceIdType.MESH
FIELDS = 8
GROUP = 12


def parts(values, count):
    out = []
    for _ in range(count):
        part = values.astype(BF16).astype(F32)
        out.append(part)
        values = values - part
    return out


def pack_kernel(lon_count, cap, half, cols, tile_ref, cell_ref, index_ref, obs_ref, prec_ref, out_ref):
    steps, count, _ = tile_ref.shape
    tile_count = out_ref.shape[0]
    me = lax.axis_index("lat") * lon_count + lax.axis_index("lon")
    base = lax.rem(me, 128 // cap) * cap
    col_bits = cols.bit_length() - 1
    half_bits = half.bit_length() - 1
    row_id = lax.broadcasted_iota(jnp.int32, (count, count), 0)
    col_id = lax.broadcasted_iota(jnp.int32, (count, count), 1)
    before = (col_id < row_id).astype(F32).astype(BF16)
    lane_id = lax.broadcasted_iota(jnp.int32, (count, 128), 1)
    wide = 1024
    wide_id = lax.broadcasted_iota(jnp.int32, (count, wide), 1)
    for step in range(steps):
        tile = tile_ref[step]
        named = (lane_id == tile).astype(F32)
        ahead = jnp.dot(before, named.astype(BF16), preferred_element_type=F32)
        rank = jnp.sum(ahead * named, axis=1, keepdims=True).astype(jnp.int32)
        lane = tile * 128 + base + rank
        cell = cell_ref[pl.ds(step, 1), :]
        row = lax.shift_right_logical(cell, col_bits)
        place = lax.shift_right_logical(row, half_bits) * cols + (cell & (cols - 1)) + 1
        values = jnp.concatenate(
            [
                place.astype(F32),
                (row & (half - 1)).astype(F32),
                index_ref[pl.ds(step, 1), :].astype(F32),
                prec_ref[pl.ds(step, 1), :],
                obs_ref[step],
                jnp.zeros((1, count), F32),
            ],
            axis=0,
        )
        split = jnp.concatenate(parts(values, 3), axis=0).astype(BF16)
        for chunk in range(tile_count * 128 // wide):
            pick = (wide_id + chunk * wide == lane).astype(F32).astype(BF16)
            got = jnp.dot(split, pick, preferred_element_type=F32)
            got = got[:FIELDS] + got[FIELDS : 2 * FIELDS] + got[2 * FIELDS :]
            for part in range(wide // 128):
                out_ref[chunk * (wide // 128) + part, pl.ds(step * FIELDS, FIELDS), :] = got[
                    :, part * 128 : (part + 1) * 128
                ]


def window_kernel(
    lat_count,
    lon_count,
    got_ref,
    table_ref,
    transport_ref,
    mixing_ref,
    trajectory_ref,
    adjoint_ref,
    flux_ref,
    slots,
    weights,
    pieces,
    place_one,
    forcing,
    upper,
    inverse,
    center,
    row_out,
    row_in,
    col_out,
    col_in,
    send_sem,
    recv_sem,
):
    tracers, layers, rows, cols = adjoint_ref.shape
    steps = trajectory_ref.shape[0]
    half = rows // 2
    slot_count = slots.shape[1]
    lat = lax.axis_index("lat")
    lon = lax.axis_index("lon")
    east = lax.rem(lon + 1, lon_count)
    west = lax.rem(lon + lon_count - 1, lon_count)
    has_north = lat > 0
    has_south = lat < lat_count - 1

    barrier = pltpu.get_barrier_semaphore()
    for side in (east, west):
        pl.semaphore_signal(barrier, inc=1, device_id=(lat, side), device_id_type=MESH)

    @pl.when(has_north)
    def _():
        pl.semaphore_signal(barrier, inc=1, device_id=(lat - 1, lon), device_id_type=MESH)

    @pl.when(has_south)
    def _():
        pl.semaphore_signal(barrier, inc=1, device_id=(lat + 1, lon), device_id_type=MESH)

    @pl.when(jnp.logical_not(has_north))
    def _():
        row_in[:, 0] = jnp.zeros((steps, tracers, layers, cols), F32)

    @pl.when(jnp.logical_not(has_south))
    def _():
        row_in[:, 1] = jnp.zeros((steps, tracers, layers, cols), F32)

    per = got_ref.shape[0] * 128 // slot_count
    for group in range(slot_count // 128):
        total = got_ref[group * per]
        for member in range(1, per):
            total = total + got_ref[group * per + member]
        slots[:, group * 128 : (group + 1) * 128] = total

    den = 1.0 + mixing_ref[0]
    inv = 1.0 / den
    inverse[0] = inv
    upper[0] = -mixing_ref[0] * inv

    def setup(k, up):
        low = mixing_ref[k - 1]
        high = mixing_ref[k]
        inv = 1.0 / ((1.0 + low + high) + low * up)
        inverse[k] = inv
        up = -high * inv
        upper[k] = up
        return up

    up = lax.fori_loop(1, layers - 1, setup, upper[0])
    low = mixing_ref[layers - 2]
    inverse[layers - 1] = 1.0 / ((1.0 + low) + low * up)

    def middle(k, _):
        center[k] = (
            1.0 - transport_ref[0, k] - transport_ref[1, k] - transport_ref[2, k] - transport_ref[3, k]
        )
        return 0

    lax.fori_loop(0, layers, middle, 0)

    groups = layers // GROUP
    table_parts = [part.astype(BF16) for part in parts(table_ref[...], 3)]

    def observe(step):
        field = slots[step * FIELDS : (step + 1) * FIELDS, :]
        place_id = lax.broadcasted_iota(jnp.int32, (2 * cols, slot_count), 0)
        place_one[...] = (place_id == field[0:1].astype(jnp.int32) - 1).astype(F32).astype(BF16)
        half_id = lax.broadcasted_iota(jnp.int32, (half, slot_count), 0)
        mask = (half_id == field[1:2].astype(jnp.int32)).astype(F32)
        mask_short = mask.astype(BF16)
        kernel_id = lax.broadcasted_iota(jnp.int32, (table_ref.shape[1], slot_count), 0)
        kernel_one = (kernel_id == field[2:3].astype(jnp.int32)).astype(F32).astype(BF16)
        looked = [jnp.dot(part, kernel_one, preferred_element_type=F32) for part in table_parts]
        weights[...] = looked[0] + looked[1] + looked[2]

        def tracer(t, _):
            total = jnp.zeros((half, slot_count), F32)
            for group in range(groups):
                first = group * GROUP
                lhs = jnp.concatenate(
                    [
                        trajectory_ref[step, t, first : first + GROUP, :half, :].reshape(GROUP * half, cols),
                        trajectory_ref[step, t, first : first + GROUP, half:, :].reshape(GROUP * half, cols),
                    ],
                    axis=1,
                )
                sampled = jnp.dot(lhs, place_one[...], preferred_element_type=F32)
                for k in range(GROUP):
                    total = total + sampled[k * half : (k + 1) * half] * weights[first + k : first + k + 1, :]
            model = jnp.sum(total * mask, axis=0, keepdims=True)
            seen = slots[pl.ds(step * FIELDS + 4 + t, 1), :]
            scaled = (model - seen) * field[3:4]
            force = weights[...] * scaled
            big, small = parts(force, 2)
            pieces[0] = big
            pieces[1] = small
            for group in range(groups):
                first = group * GROUP
                placed = None
                for part in range(2):
                    lines = [
                        jnp.broadcast_to(
                            pieces[part, first + k : first + k + 1, :], (half, slot_count)
                        ).astype(BF16)
                        * mask_short
                        for k in range(GROUP)
                    ]
                    piece = lax.dot_general(
                        jnp.concatenate(lines, axis=0),
                        place_one[...],
                        (((1,), (1,)), ((), ())),
                        preferred_element_type=F32,
                    )
                    placed = piece if placed is None else placed + piece
                forcing[t, first : first + GROUP, :half, :] = placed[:, :cols].reshape(GROUP, half, cols)
                forcing[t, first : first + GROUP, half:, :] = placed[:, cols:].reshape(GROUP, half, cols)
            return 0

        lax.fori_loop(0, tracers, tracer, 0)

    lane = lax.broadcasted_iota(jnp.int32, (rows, cols), 1)
    line = lax.broadcasted_iota(jnp.int32, (rows, cols), 0)
    edge_pair = (lane == 0) | (lane == cols - 1)

    def vertical(first_step):
        def load(k):
            return forcing[:, k] if first_step else adjoint_ref[:, k] + forcing[:, k]

        d = load(0) * inverse[0]
        forcing[:, 0] = d

        def down(k, d):
            d = (load(k) + mixing_ref[k - 1] * d) * inverse[k]
            forcing[:, k] = d
            return d

        x = lax.fori_loop(1, layers, down, d, unroll=5)

        def back(i, x):
            k = layers - 2 - i
            x = forcing[:, k] - upper[k] * x
            forcing[:, k] = x
            return x

        lax.fori_loop(0, layers - 1, back, x, unroll=5)

    def pack(step):
        for t in range(tracers):
            def level(k, held):
                x = forcing[t, k]
                eastward = pltpu.roll(transport_ref[0, k] * x, 1, 1)
                westward = pltpu.roll(transport_ref[1, k] * x, cols - 1, 1)
                inner = center[k] * x + jnp.where(lane == 0, 0.0, eastward)
                inner = inner + jnp.where(lane == cols - 1, 0.0, westward)
                south = transport_ref[2, k] * x
                north = transport_ref[3, k] * x
                row_out[step, 0, t, pl.ds(k, 1), :] = north[0:1]
                row_out[step, 1, t, pl.ds(k, 1), :] = south[rows - 1 : rows]
                inner = inner + jnp.where(line == 0, 0.0, pltpu.roll(south, 1, 0))
                inner = inner + jnp.where(line == rows - 1, 0.0, pltpu.roll(north, rows - 1, 0))
                adjoint_ref[t, k] = inner
                both = pltpu.roll(jnp.where(lane == 0, eastward, westward), 2 * k, 1)
                here = (lane == 2 * k) | (lane == lax.rem(2 * k + cols - 1, cols))
                return jnp.where(here, both, held)

            col_out[step, t] = lax.fori_loop(0, layers, level, jnp.zeros((rows, cols), F32), unroll=4)

    def copies(step):
        north = pltpu.make_async_remote_copy(
            src_ref=row_out.at[step, 0], dst_ref=row_in.at[step, 1],
            send_sem=send_sem.at[step, 0], recv_sem=recv_sem.at[step, 1],
            device_id=(lat - 1, lon), device_id_type=MESH,
        )
        south = pltpu.make_async_remote_copy(
            src_ref=row_out.at[step, 1], dst_ref=row_in.at[step, 0],
            send_sem=send_sem.at[step, 1], recv_sem=recv_sem.at[step, 0],
            device_id=(lat + 1, lon), device_id_type=MESH,
        )
        to_east = pltpu.make_async_remote_copy(
            src_ref=col_out.at[step], dst_ref=col_in.at[step, 0],
            send_sem=send_sem.at[step, 2], recv_sem=recv_sem.at[step, 2],
            device_id=(lat, east), device_id_type=MESH,
        )
        to_west = pltpu.make_async_remote_copy(
            src_ref=col_out.at[step], dst_ref=col_in.at[step, 1],
            send_sem=send_sem.at[step, 3], recv_sem=recv_sem.at[step, 3],
            device_id=(lat, west), device_id_type=MESH,
        )
        return north, south, to_east, to_west

    def finish(step):
        for t in range(tracers):
            held = jnp.where((lane & 1) == 0, col_in[step, 0, t], col_in[step, 1, t])

            def level(k, _):
                shift = lax.rem(cols - 2 * k, cols)
                side = jnp.where(edge_pair, pltpu.roll(held, shift, 1), 0.0)
                top = jnp.where(line == 0, row_in[step, 0, t, pl.ds(k, 1), :], 0.0)
                bottom = jnp.where(line == rows - 1, row_in[step, 1, t, pl.ds(k, 1), :], 0.0)
                adjoint_ref[t, k] = adjoint_ref[t, k] + side + (top + bottom)
                return 0

            lax.fori_loop(0, layers, level, 0, unroll=4)

    count = 2 + has_north.astype(jnp.int32) + has_south.astype(jnp.int32)
    pl.semaphore_wait(barrier, count)

    observe(steps - 1)
    for step in range(steps - 1, -1, -1):
        vertical(step == steps - 1)
        pack(step)
        north, south, to_east, to_west = copies(step)
        to_east.start()
        to_west.start()

        @pl.when(has_north)
        def _():
            north.start()

        @pl.when(has_south)
        def _():
            south.start()

        if step > 0:
            observe(step - 1)

        to_east.wait()
        to_west.wait()

        @pl.when(has_north)
        def _():
            north.wait_send()
            south.wait_recv()

        @pl.when(has_south)
        def _():
            south.wait_send()
            north.wait_recv()

        finish(step)
        flux_ref[...] = adjoint_ref[:, 0] if step == steps - 1 else flux_ref[...] + adjoint_ref[:, 0]


def body(
    lat_count,
    lon_count,
    transport,
    mixing,
    trajectory,
    kernel_table,
    track_tile,
    sound_cell,
    kernel_index,
    observed,
    precision,
):
    tile_count = lat_count * lon_count
    steps, count, _ = track_tile.shape
    cap = max(2, 2 * count // tile_count)
    _, tracers, layers, rows, cols = trajectory.shape
    vmem = pl.BlockSpec(memory_space=pltpu.VMEM)
    packed = pl.pallas_call(
        functools.partial(pack_kernel, lon_count, cap, rows // 2, cols),
        out_shape=jax.ShapeDtypeStruct((tile_count, steps * FIELDS, 128), F32),
        in_specs=[vmem] * 5,
        out_specs=vmem,
        compiler_params=pltpu.CompilerParams(vmem_limit_bytes=40 << 20),
    )(track_tile, sound_cell, kernel_index, observed, precision)
    got = lax.all_to_all(packed, ("lat", "lon"), split_axis=0, concat_axis=0, tiled=True)
    slot_count = tile_count * cap
    field = (tracers, layers, rows, cols)
    return pl.pallas_call(
        functools.partial(window_kernel, lat_count, lon_count),
        out_shape=(jax.ShapeDtypeStruct(field, F32), jax.ShapeDtypeStruct((tracers, rows, cols), F32)),
        in_specs=[vmem] * 5,
        out_specs=(vmem, vmem),
        scratch_shapes=[
            pltpu.VMEM((steps * FIELDS, slot_count), F32),
            pltpu.VMEM((layers, slot_count), F32),
            pltpu.VMEM((2, layers, slot_count), F32),
            pltpu.VMEM((2 * cols, slot_count), BF16),
            pltpu.VMEM(field, F32),
            pltpu.VMEM((layers, rows, cols), F32),
            pltpu.VMEM((layers, rows, cols), F32),
            pltpu.VMEM((layers, rows, cols), F32),
            pltpu.VMEM((steps, 2, tracers, layers, cols), F32),
            pltpu.VMEM((steps, 2, tracers, layers, cols), F32),
            pltpu.VMEM((steps, tracers, rows, cols), F32),
            pltpu.VMEM((steps, 2, tracers, rows, cols), F32),
            pltpu.SemaphoreType.DMA((steps, 4)),
            pltpu.SemaphoreType.DMA((steps, 4)),
        ],
        compiler_params=pltpu.CompilerParams(
            collective_id=0, has_side_effects=True, vmem_limit_bytes=48 << 20
        ),
    )(got, kernel_table.T, transport, mixing, trajectory)


def solution(mesh):
    return jax.shard_map(
        functools.partial(body, mesh.shape["lat"], mesh.shape["lon"]),
        mesh=mesh,
        in_specs=(
            P(None, None, "lat", "lon"),
            P(None, "lat", "lon"),
            P(None, None, None, "lat", "lon"),
            P(),
            P(None, ("lat", "lon"), None),
            P(None, ("lat", "lon")),
            P(None, ("lat", "lon")),
            P(None, None, ("lat", "lon")),
            P(None, ("lat", "lon")),
        ),
        out_specs=(P(None, None, "lat", "lon"), P(None, "lat", "lon")),
        check_vma=False,
    )
```

profile of v0, /device:TPU:0, one launch (start us, length us, event | category | flops | bytes accessed | tf_op | source)
XLA Modules:
  0.0 96.6 jit_solution(3942131737670157776)
XLA Ops:
  0.6 0.0 copy-start.2
  0.6 0.0 copy-start
  0.6 0.9 copy.12.obs_ref
  1.6 1.1 %copy.11.tile_ref = s32[4,512,1]{2,1,0:T(8,128)S(1)} copy(s32[4,512,1]{1,2,0:T(1,128)} %param.13) | data formatting | bytes 16384 | tf_op args[4]
  2.6 0.0 copy-start.3
  2.6 0.7 copy-done.3
  3.3 0.0 copy-start.4
  3.3 0.7 copy-done.4
  4.0 0.0 copy-start.5
  4.0 0.7 copy-done.5
  4.7 0.0 copy-start.1
  4.7 5.8 %shard_map.104 = f32[32,32,128]{2,1,0:T(8,128)S(1)} custom-call(s32[4,512,1]{2,1,0:T(8,128)S(1)} %copy.11.tile_ref, s32[4,512]{1,0:T(4,128)S(1)} %copy-done.3, s32[4,512]{1,0:T(4,128)S(1)} %copy-done.4, f32[4,3,512]{2,1,0:T(4,128)S(1)} %copy.12.obs_ref, f32[4,512]{1,0:T(4,128)S(1)} %copy-done.5), custom_call_target="tpu_custom_call" | custom-call | tf_op jit(solution)/shard_map/pallas_call | solution.py:360
  10.5 23.5 %all_to_all.5.got_ref = f32[32,32,128]{2,1,0:T(8,128)S(1)} all-to-all(f32[32,32,128]{2,1,0:T(8,128)S(1)} %shard_map.104), channel_id=1, replica_groups=mesh['lat'=4,'lon'=8] {'lat','lon'}, dimensions={0} | all-to-all | bytes 1048576 | tf_op jit(solution)/shard_map/all_to_all | solution.py:367
  34.0 0.0 copy-done.2
  34.0 0.0 copy-done
  34.0 0.0 copy-done.1
  34.0 60.7 %shard_map.105 = (f32[3,36,32,128]{3,2,1,0:T(8,128)S(1)}, f32[3,32,128]{2,1,0:T(8,128)S(1)}) custom-call(f32[32,32,128]{2,1,0:T(8,128)S(1)} %all_to_all.5.got_ref, f32[36,64]{1,0:T(8,128)S(1)} %bitcast.1, f32[4,36,32,128]{3,2,1,0:T(8,128)S(1)} %copy-done, f32[35,32,128]{2,1,0:T(8,128)S(1)} %copy-done.1, bf16[4,3,36,32,128]{4,3,2,1,0:T(8,128)(2,1)} %trajectory_ref.1), custom_call_target="tpu_custom_call" | custom-call | tf_op jit(solution)/shard_map/pallas_call | solution.py:370
  94.7 1.2 %copy.15 = f32[3,36,32,128]{3,2,1,0:T(8,128)} copy(f32[3,36,32,128]{3,2,1,0:T(8,128)S(1)} %get-tuple-element.4) | data formatting | bytes 3538944
  96.0 0.6 copy.16
Async XLA Ops:
  0.6 33.4 %copy-start.2 = (f32[64,36]{0,1:T(8,128)S(1)}, f32[64,36]{0,1:T(8,128)}, u32[]{:S(2)}) copy-start(f32[64,36]{0,1:T(8,128)} %param.12) | copy-start | bytes 27652
  0.6 33.4 %copy-start = (f32[4,36,32,128]{3,2,1,0:T(8,128)S(1)}, f32[4,36,32,128]{3,2,1,0:T(8,128)}, u32[]{:S(2)}) copy-start(f32[4,36,32,128]{3,2,1,0:T(8,128)} %transport_ref.1) | copy-start | bytes 7077892
  2.6 0.7 copy-start.3
  3.3 0.7 copy-start.4
  4.0 0.7 copy-start.5
  4.7 29.3 %copy-start.1 = (f32[35,32,128]{2,1,0:T(8,128)S(1)}, f32[35,32,128]{2,1,0:T(8,128)}, u32[]{:S(2)}) copy-start(f32[35,32,128]{2,1,0:T(8,128)} %mixing_ref.1) | copy-start | bytes 1720324
where the time goes:
time: 97 us; the launch traced here: 96.6 us
  Pallas kernels  66.5 us (69%)
  blocking collectives  23.5 us (24%)
  local copies, waits for them, and re-layouts  5.89 us (6%)
    pallas_call x1, Pallas kernels, body(): pl.pallas_call(functools.partial(window_kernel, lat_count, lon_count), ou...  60.7 us
    all_to_all x1, blocking collectives, body(): lax.all_to_all(packed, ('lat', 'lon'), split_axis=0, concat_axis=0, tiled...  23.5 us
    unnamed x16, local copies, waits for them, and re-layouts  5.89 us
    pallas_call x1, Pallas kernels, body(): pl.pallas_call(functools.partial(pack_kernel, lon_count, cap, rows // 2,...  5.81 us

commit v1 on v0

--- a/solution.py
+++ b/solution.py
@@ -11,7 +11,6 @@
 BF16 = jnp.bfloat16
 MESH = pl.DeviceIdType.MESH
 FIELDS = 8
-GROUP = 12
 
 
 def parts(values, count):
@@ -23,25 +22,29 @@
     return out
 
 
-def pack_kernel(lon_count, cap, half, cols, tile_ref, cell_ref, index_ref, obs_ref, prec_ref, out_ref):
-    steps, count, _ = tile_ref.shape
+def pack_kernel(cap, half, cols, tile_ref, cell_ref, index_ref, obs_ref, prec_ref, out_ref):
+    steps, count = tile_ref.shape
     tile_count = out_ref.shape[0]
-    me = lax.axis_index("lat") * lon_count + lax.axis_index("lon")
-    base = lax.rem(me, 128 // cap) * cap
+    slot_count = tile_count * cap
     col_bits = cols.bit_length() - 1
     half_bits = half.bit_length() - 1
     row_id = lax.broadcasted_iota(jnp.int32, (count, count), 0)
     col_id = lax.broadcasted_iota(jnp.int32, (count, count), 1)
-    before = (col_id < row_id).astype(F32).astype(BF16)
-    lane_id = lax.broadcasted_iota(jnp.int32, (count, 128), 1)
-    wide = 1024
-    wide_id = lax.broadcasted_iota(jnp.int32, (count, wide), 1)
+    before = (row_id < col_id).astype(F32).astype(BF16)
+    tile_id = lax.broadcasted_iota(jnp.int32, (tile_count, count), 0)
+    slot_id = lax.broadcasted_iota(jnp.int32, (count, slot_count), 1)
+    lane = lax.broadcasted_iota(jnp.int32, (FIELDS, 128), 1)
+    slots = []
     for step in range(steps):
-        tile = tile_ref[step]
-        named = (lane_id == tile).astype(F32)
-        ahead = jnp.dot(before, named.astype(BF16), preferred_element_type=F32)
-        rank = jnp.sum(ahead * named, axis=1, keepdims=True).astype(jnp.int32)
-        lane = tile * 128 + base + rank
+        tile = tile_ref[pl.ds(step, 1), :]
+        named = (tile_id == tile).astype(F32)
+        ahead = jnp.dot(named.astype(BF16), before, preferred_element_type=F32)
+        rank = jnp.sum(ahead * named, axis=0, keepdims=True)
+        slots.append((tile * cap).astype(F32) + rank)
+    slots.append(jnp.zeros((8 - steps, count), F32))
+    slot_columns = jnp.concatenate(slots, axis=0).T.astype(jnp.int32)
+    blocks = [jnp.zeros((FIELDS, 128), F32)] * tile_count
+    for step in range(steps):
         cell = cell_ref[pl.ds(step, 1), :]
         row = lax.shift_right_logical(cell, col_bits)
         place = lax.shift_right_logical(row, half_bits) * cols + (cell & (cols - 1)) + 1
@@ -57,14 +60,19 @@
             axis=0,
         )
         split = jnp.concatenate(parts(values, 3), axis=0).astype(BF16)
-        for chunk in range(tile_count * 128 // wide):
-            pick = (wide_id + chunk * wide == lane).astype(F32).astype(BF16)
-            got = jnp.dot(split, pick, preferred_element_type=F32)
-            got = got[:FIELDS] + got[FIELDS : 2 * FIELDS] + got[2 * FIELDS :]
-            for part in range(wide // 128):
-                out_ref[chunk * (wide // 128) + part, pl.ds(step * FIELDS, FIELDS), :] = got[
-                    :, part * 128 : (part + 1) * 128
-                ]
+        pick = (slot_id == slot_columns[:, step : step + 1]).astype(F32).astype(BF16)
+        got = jnp.dot(split, pick, preferred_element_type=F32)
+        got = got[:FIELDS] + got[FIELDS : 2 * FIELDS] + got[2 * FIELDS :]
+        here = (lane >= step * cap) & (lane < (step + 1) * cap)
+        for tile in range(tile_count):
+            first = tile * cap // 128 * 128
+            piece = got[:, first : first + 128]
+            shift = (step * cap + first - tile * cap) % 128
+            if shift:
+                piece = pltpu.roll(piece, shift, 1)
+            blocks[tile] = jnp.where(here, piece, blocks[tile])
+    for tile in range(tile_count):
+        out_ref[tile] = blocks[tile]
 
 
 def window_kernel(
@@ -81,6 +89,8 @@
     weights,
     pieces,
     place_one,
+    place_turned,
+    masked,
     forcing,
     upper,
     inverse,
@@ -124,11 +134,19 @@
         row_in[:, 1] = jnp.zeros((steps, tracers, layers, cols), F32)
 
     per = got_ref.shape[0] * 128 // slot_count
+    cap = 128 // per
+    slot_lane = lax.broadcasted_iota(jnp.int32, (FIELDS, 128), 1)
     for group in range(slot_count // 128):
-        total = got_ref[group * per]
-        for member in range(1, per):
-            total = total + got_ref[group * per + member]
-        slots[:, group * 128 : (group + 1) * 128] = total
+        for step in range(steps):
+            total = jnp.zeros((FIELDS, 128), F32)
+            for member in range(per):
+                block = got_ref[group * per + member]
+                shift = (member - step) * cap % 128
+                if shift:
+                    block = pltpu.roll(block, shift, 1)
+                here = (slot_lane >= member * cap) & (slot_lane < (member + 1) * cap)
+                total = jnp.where(here, block, total)
+            slots[step * FIELDS : (step + 1) * FIELDS, group * 128 : (group + 1) * 128] = total
 
     den = 1.0 + mixing_ref[0]
     inv = 1.0 / den
@@ -156,13 +174,15 @@
 
     lax.fori_loop(0, layers, middle, 0)
 
-    groups = layers // GROUP
     table_parts = [part.astype(BF16) for part in parts(table_ref[...], 3)]
+    channel = layers * half
 
     def observe(step):
         field = slots[step * FIELDS : (step + 1) * FIELDS, :]
         place_id = lax.broadcasted_iota(jnp.int32, (2 * cols, slot_count), 0)
-        place_one[...] = (place_id == field[0:1].astype(jnp.int32) - 1).astype(F32).astype(BF16)
+        one = (place_id == field[0:1].astype(jnp.int32) - 1).astype(F32).astype(BF16)
+        place_one[...] = one
+        place_turned[...] = one.T
         half_id = lax.broadcasted_iota(jnp.int32, (half, slot_count), 0)
         mask = (half_id == field[1:2].astype(jnp.int32)).astype(F32)
         mask_short = mask.astype(BF16)
@@ -171,50 +191,32 @@
         looked = [jnp.dot(part, kernel_one, preferred_element_type=F32) for part in table_parts]
         weights[...] = looked[0] + looked[1] + looked[2]
 
-        def tracer(t, _):
+        for t in range(tracers):
+            lhs = jnp.concatenate(
+                [
+                    trajectory_ref[step, t, :, :half, :].reshape(channel, cols),
+                    trajectory_ref[step, t, :, half:, :].reshape(channel, cols),
+                ],
+                axis=1,
+            )
+            sampled = jnp.dot(lhs, place_one[...], preferred_element_type=F32)
             total = jnp.zeros((half, slot_count), F32)
-            for group in range(groups):
-                first = group * GROUP
-                lhs = jnp.concatenate(
-                    [
-                        trajectory_ref[step, t, first : first + GROUP, :half, :].reshape(GROUP * half, cols),
-                        trajectory_ref[step, t, first : first + GROUP, half:, :].reshape(GROUP * half, cols),
-                    ],
-                    axis=1,
-                )
-                sampled = jnp.dot(lhs, place_one[...], preferred_element_type=F32)
-                for k in range(GROUP):
-                    total = total + sampled[k * half : (k + 1) * half] * weights[first + k : first + k + 1, :]
+            for k in range(layers):
+                total = total + sampled[k * half : (k + 1) * half] * weights[k : k + 1, :]
             model = jnp.sum(total * mask, axis=0, keepdims=True)
-            seen = slots[pl.ds(step * FIELDS + 4 + t, 1), :]
-            scaled = (model - seen) * field[3:4]
-            force = weights[...] * scaled
-            big, small = parts(force, 2)
-            pieces[0] = big
-            pieces[1] = small
-            for group in range(groups):
-                first = group * GROUP
-                placed = None
-                for part in range(2):
-                    lines = [
-                        jnp.broadcast_to(
-                            pieces[part, first + k : first + k + 1, :], (half, slot_count)
-                        ).astype(BF16)
-                        * mask_short
-                        for k in range(GROUP)
-                    ]
-                    piece = lax.dot_general(
-                        jnp.concatenate(lines, axis=0),
-                        place_one[...],
-                        (((1,), (1,)), ((), ())),
-                        preferred_element_type=F32,
-                    )
-                    placed = piece if placed is None else placed + piece
-                forcing[t, first : first + GROUP, :half, :] = placed[:, :cols].reshape(GROUP, half, cols)
-                forcing[t, first : first + GROUP, half:, :] = placed[:, cols:].reshape(GROUP, half, cols)
-            return 0
-
-        lax.fori_loop(0, tracers, tracer, 0)
+            scaled = (model - field[4 + t : 5 + t]) * field[3:4]
+            big, small = parts(weights[...] * scaled, 2)
+            pieces[t, 0] = big
+            pieces[t, 1] = small
+            for part in range(2):
+                for k in range(layers):
+                    first = part * channel + k * half
+                    line = jnp.broadcast_to(pieces[t, part, k : k + 1, :], (half, slot_count))
+                    masked[t, first : first + half, :] = line.astype(BF16) * mask_short
+            placed = jnp.dot(masked[t], place_turned[...], preferred_element_type=F32)
+            placed = placed[:channel] + placed[channel:]
+            forcing[t, :, :half, :] = placed[:, :cols].reshape(layers, half, cols)
+            forcing[t, :, half:, :] = placed[:, cols:].reshape(layers, half, cols)
 
     lane = lax.broadcasted_iota(jnp.int32, (rows, cols), 1)
     line = lax.broadcasted_iota(jnp.int32, (rows, cols), 0)
@@ -358,12 +360,12 @@
     _, tracers, layers, rows, cols = trajectory.shape
     vmem = pl.BlockSpec(memory_space=pltpu.VMEM)
     packed = pl.pallas_call(
-        functools.partial(pack_kernel, lon_count, cap, rows // 2, cols),
-        out_shape=jax.ShapeDtypeStruct((tile_count, steps * FIELDS, 128), F32),
+        functools.partial(pack_kernel, cap, rows // 2, cols),
+        out_shape=jax.ShapeDtypeStruct((tile_count, FIELDS, 128), F32),
         in_specs=[vmem] * 5,
         out_specs=vmem,
         compiler_params=pltpu.CompilerParams(vmem_limit_bytes=40 << 20),
-    )(track_tile, sound_cell, kernel_index, observed, precision)
+    )(track_tile[:, :, 0], sound_cell, kernel_index, observed, precision)
     got = lax.all_to_all(packed, ("lat", "lon"), split_axis=0, concat_axis=0, tiled=True)
     slot_count = tile_count * cap
     field = (tracers, layers, rows, cols)
@@ -375,8 +377,10 @@
         scratch_shapes=[
             pltpu.VMEM((steps * FIELDS, slot_count), F32),
             pltpu.VMEM((layers, slot_count), F32),
-            pltpu.VMEM((2, layers, slot_count), F32),
+            pltpu.VMEM((tracers, 2, layers, slot_count), F32),
             pltpu.VMEM((2 * cols, slot_count), BF16),
+            pltpu.VMEM((slot_count, 2 * cols), BF16),
+            pltpu.VMEM((tracers, layers * rows, slot_count), BF16),
             pltpu.VMEM(field, F32),
             pltpu.VMEM((layers, rows, cols), F32),
             pltpu.VMEM((layers, rows, cols), F32),

time: 97 us -> 84.3 us (0.87)
  blocking collectives: 23.5 us -> 14.8 us
  Pallas kernels: 66.5 us -> 59.4 us
  local copies, waits for them, and re-layouts: 5.89 us -> 8.82 us
    all_to_all x1, blocking collectives: 23.5 us -> 14.8 us  [body(): lax.all_to_all(packed, ('lat', 'lon'), split_axis=0, concat_axis=0, tiled...]
    pallas_call x1, Pallas kernels: 5.81 us -> 1.63 us  [body(): pl.pallas_call(functools.partial(pack_kernel, cap, rows // 2, cols), out_...]
    pallas_call x1, Pallas kernels: 60.7 us -> 57.8 us  [body(): pl.pallas_call(functools.partial(window_kernel, lat_count, lon_count), ou...]
    unnamed x16, local copies, waits for them, and re-layouts: 5.89 us -> 8.82 us
where the time goes in v1:
time: 84.3 us; the launch traced here: 83.7 us
  Pallas kernels  59.4 us (70%)
  blocking collectives  14.8 us (18%)
  local copies, waits for them, and re-layouts  8.82 us (10%)
    pallas_call x1, Pallas kernels, body(): pl.pallas_call(functools.partial(window_kernel, lat_count, lon_count), ou...  57.8 us
    all_to_all x1, blocking collectives, body(): lax.all_to_all(packed, ('lat', 'lon'), split_axis=0, concat_axis=0, tiled...  14.8 us
    unnamed x16, local copies, waits for them, and re-layouts  8.82 us

profile of v1, /device:TPU:0, one launch (start us, length us, event | category | flops | bytes accessed | tf_op | source)
XLA Modules:
  0.0 83.7 jit_solution(6123076647686049791)
XLA Ops:
  0.6 0.7 copy.14
  1.3 0.8 copy.11.obs_ref
  2.1 0.0 copy-start.3
  2.1 0.7 copy-done.3
  2.8 0.0 copy-start.4
  2.8 0.7 copy-done.4
  3.5 0.0 copy-start.5
  3.5 0.7 copy-done.5
  4.2 1.6 %shard_map.104 = f32[32,8,128]{2,1,0:T(8,128)S(1)} custom-call(s32[4,512]{1,0:T(4,128)S(1)} %bitcast.4, s32[4,512]{1,0:T(4,128)S(1)} %copy-done.3, s32[4,512]{1,0:T(4,128)S(1)} %copy-done.4, f32[4,3,512]{2,1,0:T(4,128)S(1)} %copy.11.obs_ref, f32[4,512]{1,0:T(4,128)S(1)} %copy-done.5), custom_call_target="tpu_custom_call" | custom-call | tf_op jit(solution)/shard_map/pallas_call | solution.py:362
  5.8 14.8 %all_to_all.5.got_ref = f32[32,8,128]{2,1,0:T(8,128)S(1)} all-to-all(f32[32,8,128]{2,1,0:T(8,128)S(1)} %shard_map.104), channel_id=1, replica_groups=mesh['lat'=4,'lon'=8] {'lat','lon'}, dimensions={0} | all-to-all | bytes 262144 | tf_op jit(solution)/shard_map/all_to_all | solution.py:369
  20.7 0.0 copy-start
  20.7 1.7 %copy-done = f32[4,36,32,128]{3,2,1,0:T(8,128)S(1)} copy-done((f32[4,36,32,128]{3,2,1,0:T(8,128)S(1)}, f32[4,36,32,128]{3,2,1,0:T(8,128)}, u32[]{:S(2)}) %copy-start) | copy-done | bytes 2359320
  22.3 0.0 copy-start.1
  22.3 1.1 %copy-done.1 = f32[35,32,128]{2,1,0:T(8,128)S(1)} copy-done((f32[35,32,128]{2,1,0:T(8,128)S(1)}, f32[35,32,128]{2,1,0:T(8,128)}, u32[]{:S(2)}) %copy-start.1) | copy-done | bytes 573464
  23.4 0.0 copy-start.2
  23.4 0.7 copy-done.2
  24.1 57.8 %shard_map.105 = (f32[3,36,32,128]{3,2,1,0:T(8,128)S(1)}, f32[3,32,128]{2,1,0:T(8,128)S(1)}) custom-call(f32[32,8,128]{2,1,0:T(8,128)S(1)} %all_to_all.5.got_ref, f32[36,64]{1,0:T(8,128)S(1)} %bitcast.5, f32[4,36,32,128]{3,2,1,0:T(8,128)S(1)} %copy-done, f32[35,32,128]{2,1,0:T(8,128)S(1)} %copy-done.1, bf16[4,3,36,32,128]{4,3,2,1,0:T(8,128)(2,1)} %trajectory_ref.1), custom_call_target="tpu_custom_call" | custom-call | tf_op jit(solution)/shard_map/pallas_call | solution.py:372
  81.9 1.2 %copy.17 = f32[3,36,32,128]{3,2,1,0:T(8,128)} copy(f32[3,36,32,128]{3,2,1,0:T(8,128)S(1)} %get-tuple-element.4) | data formatting | bytes 3538944
  83.1 0.6 copy.18
Async XLA Ops:
  2.1 0.7 copy-start.3
  2.8 0.7 copy-start.4
  3.5 0.7 copy-start.5
  20.7 1.7 %copy-start = (f32[4,36,32,128]{3,2,1,0:T(8,128)S(1)}, f32[4,36,32,128]{3,2,1,0:T(8,128)}, u32[]{:S(2)}) copy-start(f32[4,36,32,128]{3,2,1,0:T(8,128)} %transport_ref.1) | copy-start | bytes 7077892
  22.3 1.1 %copy-start.1 = (f32[35,32,128]{2,1,0:T(8,128)S(1)}, f32[35,32,128]{2,1,0:T(8,128)}, u32[]{:S(2)}) copy-start(f32[35,32,128]{2,1,0:T(8,128)} %mixing_ref.1) | copy-start | bytes 1720324
  23.4 0.7 copy-start.2

commit v2 on v1

--- a/solution.py
+++ b/solution.py
@@ -99,6 +99,7 @@
     row_in,
     col_out,
     col_in,
+    sides,
     send_sem,
     recv_sem,
 ):
@@ -221,49 +222,78 @@
     lane = lax.broadcasted_iota(jnp.int32, (rows, cols), 1)
     line = lax.broadcasted_iota(jnp.int32, (rows, cols), 0)
     edge_pair = (lane == 0) | (lane == cols - 1)
-
-    def vertical(first_step):
-        def load(k):
-            return forcing[:, k] if first_step else adjoint_ref[:, k] + forcing[:, k]
-
-        d = load(0) * inverse[0]
-        forcing[:, 0] = d
-
-        def down(k, d):
-            d = (load(k) + mixing_ref[k - 1] * d) * inverse[k]
-            forcing[:, k] = d
-            return d
-
-        x = lax.fori_loop(1, layers, down, d, unroll=5)
-
-        def back(i, x):
-            k = layers - 2 - i
-            x = forcing[:, k] - upper[k] * x
-            forcing[:, k] = x
-            return x
-
-        lax.fori_loop(0, layers - 1, back, x, unroll=5)
-
-    def pack(step):
+    line_eight = lax.broadcasted_iota(jnp.int32, (8, cols), 0)
+    upper[layers - 1] = jnp.zeros((rows, cols), F32)
+
+    def merge(step):
         for t in range(tracers):
-            def level(k, held):
-                x = forcing[t, k]
-                eastward = pltpu.roll(transport_ref[0, k] * x, 1, 1)
-                westward = pltpu.roll(transport_ref[1, k] * x, cols - 1, 1)
-                inner = center[k] * x + jnp.where(lane == 0, 0.0, eastward)
-                inner = inner + jnp.where(lane == cols - 1, 0.0, westward)
+            from_east = pltpu.roll(col_in[step, 1, t], cols - 2, 1)
+            sides[t] = jnp.where((lane & 1) == 0, col_in[step, 0, t], from_east)
+
+    def arrived(step, t, k):
+        side = jnp.where(edge_pair, pltpu.roll(sides[t], lax.rem(cols - 2 * k, cols), 1), 0.0)
+        full = adjoint_ref[t, k] + side
+        top = jnp.where(line_eight == 0, row_in[step, 0, t, pl.ds(k, 1), :], 0.0)
+        bottom = jnp.where(line_eight == 7, row_in[step, 1, t, pl.ds(k, 1), :], 0.0)
+        return jnp.concatenate([full[:8] + top, full[8 : rows - 8], full[rows - 8 :] + bottom], axis=0)
+
+    def add_flux(t, value, first_step):
+        flux_ref[t] = value if first_step else flux_ref[t] + value
+
+    def sweep_up(step):
+        first = step == steps - 1
+
+        def load(t, k):
+            return forcing[t, k] if first else arrived(step + 1, t, k) + forcing[t, k]
+
+        start = []
+        for t in range(tracers):
+            value = forcing[t, 0]
+            if not first:
+                before = arrived(step + 1, t, 0)
+                add_flux(t, before, step == steps - 2)
+                value = value + before
+            start.append(value * inverse[0])
+            forcing[t, 0] = start[-1]
+
+        def level(k, held):
+            out = []
+            for t in range(tracers):
+                d = (load(t, k) + mixing_ref[k - 1] * held[t]) * inverse[k]
+                forcing[t, k] = d
+                out.append(d)
+            return tuple(out)
+
+        lax.fori_loop(1, layers, level, tuple(start), unroll=5)
+
+    def sweep_down(step):
+        def level(i, carry):
+            k = layers - 1 - i
+            xs, packed = carry
+            new_xs, new_packed = [], []
+            here = (lane == 2 * k) | (lane == 2 * k + 1)
+            for t in range(tracers):
+                x = forcing[t, k] - upper[k] * xs[t]
+                eastward = transport_ref[0, k] * x
+                westward = transport_ref[1, k] * x
                 south = transport_ref[2, k] * x
                 north = transport_ref[3, k] * x
                 row_out[step, 0, t, pl.ds(k, 1), :] = north[0:1]
                 row_out[step, 1, t, pl.ds(k, 1), :] = south[rows - 1 : rows]
+                both = pltpu.roll(jnp.where(lane == cols - 1, eastward, westward), 2 * k + 1, 1)
+                inner = center[k] * x + jnp.where(lane == 0, 0.0, pltpu.roll(eastward, 1, 1))
+                inner = inner + jnp.where(lane == cols - 1, 0.0, pltpu.roll(westward, cols - 1, 1))
                 inner = inner + jnp.where(line == 0, 0.0, pltpu.roll(south, 1, 0))
                 inner = inner + jnp.where(line == rows - 1, 0.0, pltpu.roll(north, rows - 1, 0))
                 adjoint_ref[t, k] = inner
-                both = pltpu.roll(jnp.where(lane == 0, eastward, westward), 2 * k, 1)
-                here = (lane == 2 * k) | (lane == lax.rem(2 * k + cols - 1, cols))
-                return jnp.where(here, both, held)
-
-            col_out[step, t] = lax.fori_loop(0, layers, level, jnp.zeros((rows, cols), F32), unroll=4)
+                new_xs.append(x)
+                new_packed.append(jnp.where(here, both, packed[t]))
+            return tuple(new_xs), tuple(new_packed)
+
+        zeros = (jnp.zeros((rows, cols), F32),) * tracers
+        _, packed = lax.fori_loop(0, layers, level, (zeros, zeros), unroll=4)
+        for t in range(tracers):
+            col_out[step, t] = packed[t]
 
     def copies(step):
         north = pltpu.make_async_remote_copy(
@@ -290,25 +320,24 @@
 
     def finish(step):
         for t in range(tracers):
-            held = jnp.where((lane & 1) == 0, col_in[step, 0, t], col_in[step, 1, t])
-
-            def level(k, _):
-                shift = lax.rem(cols - 2 * k, cols)
-                side = jnp.where(edge_pair, pltpu.roll(held, shift, 1), 0.0)
-                top = jnp.where(line == 0, row_in[step, 0, t, pl.ds(k, 1), :], 0.0)
-                bottom = jnp.where(line == rows - 1, row_in[step, 1, t, pl.ds(k, 1), :], 0.0)
-                adjoint_ref[t, k] = adjoint_ref[t, k] + side + (top + bottom)
-                return 0
-
-            lax.fori_loop(0, layers, level, 0, unroll=4)
+            value = arrived(step, t, 0)
+            adjoint_ref[t, 0] = value
+            add_flux(t, value, step == steps - 1)
+
+        def level(k, _):
+            for t in range(tracers):
+                adjoint_ref[t, k] = arrived(step, t, k)
+            return 0
+
+        lax.fori_loop(1, layers, level, 0, unroll=5)
 
     count = 2 + has_north.astype(jnp.int32) + has_south.astype(jnp.int32)
     pl.semaphore_wait(barrier, count)
 
     observe(steps - 1)
     for step in range(steps - 1, -1, -1):
-        vertical(step == steps - 1)
-        pack(step)
+        sweep_up(step)
+        sweep_down(step)
         north, south, to_east, to_west = copies(step)
         to_east.start()
         to_west.start()
@@ -337,8 +366,8 @@
             south.wait_send()
             north.wait_recv()
 
-        finish(step)
-        flux_ref[...] = adjoint_ref[:, 0] if step == steps - 1 else flux_ref[...] + adjoint_ref[:, 0]
+        merge(step)
+    finish(0)
 
 
 def body(
@@ -389,6 +418,7 @@
             pltpu.VMEM((steps, 2, tracers, layers, cols), F32),
             pltpu.VMEM((steps, tracers, rows, cols), F32),
             pltpu.VMEM((steps, 2, tracers, rows, cols), F32),
+            pltpu.VMEM((tracers, rows, cols), F32),
             pltpu.SemaphoreType.DMA((steps, 4)),
             pltpu.SemaphoreType.DMA((steps, 4)),
         ],

time: 84.3 us -> 66.6 us (0.79)
  Pallas kernels: 59.4 us -> 41.7 us
    pallas_call x1, Pallas kernels: 57.8 us -> 40.1 us  [body(): pl.pallas_call(functools.partial(window_kernel, lat_count, lon_count), ou...]
where the time goes in v2:
time: 66.6 us; the launch traced here: 66 us
  Pallas kernels  41.7 us (63%)
  blocking collectives  14.8 us (22%)
  local copies, waits for them, and re-layouts  8.82 us (13%)
    pallas_call x1, Pallas kernels, body(): pl.pallas_call(functools.partial(window_kernel, lat_count, lon_count), ou...  40.1 us
    all_to_all x1, blocking collectives, body(): lax.all_to_all(packed, ('lat', 'lon'), split_axis=0, concat_axis=0, tiled...  14.8 us
    unnamed x16, local copies, waits for them, and re-layouts  8.82 us
    pallas_call x1, Pallas kernels, body(): pl.pallas_call(functools.partial(pack_kernel, cap, rows // 2, cols), out_...  1.63 us

profile of v2, /device:TPU:0, one launch (start us, length us, event | category | flops | bytes accessed | tf_op | source)
XLA Modules:
  0.0 66.0 jit_solution(1148175634153179025)
XLA Ops:
  0.6 0.7 %copy.14 = s32[4,512,1]{1,0,2:T(4,128)S(1)} copy(s32[4,512,1]{1,2,0:T(1,128)} %param.13) | data formatting | bytes 16384
  1.3 0.8 %copy.11.obs_ref = f32[4,3,512]{2,1,0:T(4,128)S(1)} copy(f32[4,3,512]{2,0,1:T(4,128)} %param.16) | data formatting | bytes 49152 | tf_op args[7]
  2.1 0.0 copy-start.3
  2.1 0.7 %copy-done.3 = s32[4,512]{1,0:T(4,128)S(1)} copy-done((s32[4,512]{1,0:T(4,128)S(1)}, s32[4,512]{1,0:T(4,128)}, u32[]{:S(2)}) %copy-start.3) | copy-done | bytes 8216
  2.8 0.0 copy-start.4
  2.8 0.7 %copy-done.4 = s32[4,512]{1,0:T(4,128)S(1)} copy-done((s32[4,512]{1,0:T(4,128)S(1)}, s32[4,512]{1,0:T(4,128)}, u32[]{:S(2)}) %copy-start.4) | copy-done | bytes 8216
  3.5 0.0 copy-start.5
  3.5 0.7 %copy-done.5 = f32[4,512]{1,0:T(4,128)S(1)} copy-done((f32[4,512]{1,0:T(4,128)S(1)}, f32[4,512]{1,0:T(4,128)}, u32[]{:S(2)}) %copy-start.5) | copy-done | bytes 8216
  4.2 1.6 %shard_map.104 = f32[32,8,128]{2,1,0:T(8,128)S(1)} custom-call(s32[4,512]{1,0:T(4,128)S(1)} %bitcast.4, s32[4,512]{1,0:T(4,128)S(1)} %copy-done.3, s32[4,512]{1,0:T(4,128)S(1)} %copy-done.4, f32[4,3,512]{2,1,0:T(4,128)S(1)} %copy.11.obs_ref, f32[4,512]{1,0:T(4,128)S(1)} %copy-done.5), custom_call_target="tpu_custom_call" | custom-call | tf_op jit(solution)/shard_map/pallas_call | solution.py:391
  5.8 14.8 %all_to_all.5.got_ref = f32[32,8,128]{2,1,0:T(8,128)S(1)} all-to-all(f32[32,8,128]{2,1,0:T(8,128)S(1)} %shard_map.104), channel_id=1, replica_groups=mesh['lat'=4,'lon'=8] {'lat','lon'}, dimensions={0} | all-to-all | bytes 262144 | tf_op jit(solution)/shard_map/all_to_all | solution.py:398
  20.7 0.0 copy-start
  20.7 1.7 %copy-done = f32[4,36,32,128]{3,2,1,0:T(8,128)S(1)} copy-done((f32[4,36,32,128]{3,2,1,0:T(8,128)S(1)}, f32[4,36,32,128]{3,2,1,0:T(8,128)}, u32[]{:S(2)}) %copy-start) | copy-done | bytes 2359320
  22.3 0.0 copy-start.1
  22.3 1.1 %copy-done.1 = f32[35,32,128]{2,1,0:T(8,128)S(1)} copy-done((f32[35,32,128]{2,1,0:T(8,128)S(1)}, f32[35,32,128]{2,1,0:T(8,128)}, u32[]{:S(2)}) %copy-start.1) | copy-done | bytes 573464
  23.4 0.0 copy-start.2
  23.4 0.7 %copy-done.2 = f32[64,36]{0,1:T(8,128)S(1)} copy-done((f32[64,36]{0,1:T(8,128)S(1)}, f32[64,36]{0,1:T(8,128)}, u32[]{:S(2)}) %copy-start.2) | copy-done | bytes 9240
  24.1 40.1 %shard_map.105 = (f32[3,36,32,128]{3,2,1,0:T(8,128)S(1)}, f32[3,32,128]{2,1,0:T(8,128)S(1)}) custom-call(f32[32,8,128]{2,1,0:T(8,128)S(1)} %all_to_all.5.got_ref, f32[36,64]{1,0:T(8,128)S(1)} %bitcast.5, f32[4,36,32,128]{3,2,1,0:T(8,128)S(1)} %copy-done, f32[35,32,128]{2,1,0:T(8,128)S(1)} %copy-done.1, bf16[4,3,36,32,128]{4,3,2,1,0:T(8,128)(2,1)} %trajectory_ref.1), custom_call_target="tpu_custom_call" | custom-call | tf_op jit(solution)/shard_map/pallas_call | solution.py:401
  64.2 1.2 %copy.17 = f32[3,36,32,128]{3,2,1,0:T(8,128)} copy(f32[3,36,32,128]{3,2,1,0:T(8,128)S(1)} %get-tuple-element.4) | data formatting | bytes 3538944
  65.4 0.6 copy.18
Async XLA Ops:
  2.1 0.7 %copy-start.3 = (s32[4,512]{1,0:T(4,128)S(1)}, s32[4,512]{1,0:T(4,128)}, u32[]{:S(2)}) copy-start(s32[4,512]{1,0:T(4,128)} %cell_ref.1) | copy-start | bytes 24580
  2.8 0.7 %copy-start.4 = (s32[4,512]{1,0:T(4,128)S(1)}, s32[4,512]{1,0:T(4,128)}, u32[]{:S(2)}) copy-start(s32[4,512]{1,0:T(4,128)} %index_ref.1) | copy-start | bytes 24580
  3.5 0.7 %copy-start.5 = (f32[4,512]{1,0:T(4,128)S(1)}, f32[4,512]{1,0:T(4,128)}, u32[]{:S(2)}) copy-start(f32[4,512]{1,0:T(4,128)} %prec_ref.1) | copy-start | bytes 24580
  20.7 1.7 %copy-start = (f32[4,36,32,128]{3,2,1,0:T(8,128)S(1)}, f32[4,36,32,128]{3,2,1,0:T(8,128)}, u32[]{:S(2)}) copy-start(f32[4,36,32,128]{3,2,1,0:T(8,128)} %transport_ref.1) | copy-start | bytes 7077892
  22.3 1.1 %copy-start.1 = (f32[35,32,128]{2,1,0:T(8,128)S(1)}, f32[35,32,128]{2,1,0:T(8,128)}, u32[]{:S(2)}) copy-start(f32[35,32,128]{2,1,0:T(8,128)} %mixing_ref.1) | copy-start | bytes 1720324
  23.4 0.7 %copy-start.2 = (f32[64,36]{0,1:T(8,128)S(1)}, f32[64,36]{0,1:T(8,128)}, u32[]{:S(2)}) copy-start(f32[64,36]{0,1:T(8,128)} %param.12) | copy-start | bytes 27652

commit v3 on v2

--- a/solution.py
+++ b/solution.py
@@ -78,13 +78,14 @@
 def window_kernel(
     lat_count,
     lon_count,
-    got_ref,
+    packed_ref,
     table_ref,
     transport_ref,
     mixing_ref,
     trajectory_ref,
     adjoint_ref,
     flux_ref,
+    got_ref,
     slots,
     weights,
     pieces,
@@ -102,6 +103,8 @@
     sides,
     send_sem,
     recv_sem,
+    out_sem,
+    in_sem,
 ):
     tracers, layers, rows, cols = adjoint_ref.shape
     steps = trajectory_ref.shape[0]
@@ -114,17 +117,33 @@
     has_north = lat > 0
     has_south = lat < lat_count - 1
 
+    me = lat * lon_count + lon
+    total_count = lat_count * lon_count
+
+    def place_of(j):
+        other = lax.rem(me + j, total_count)
+        return other, (lax.div(other, lon_count), lax.rem(other, lon_count))
+
     barrier = pltpu.get_barrier_semaphore()
-    for side in (east, west):
-        pl.semaphore_signal(barrier, inc=1, device_id=(lat, side), device_id_type=MESH)
-
-    @pl.when(has_north)
-    def _():
-        pl.semaphore_signal(barrier, inc=1, device_id=(lat - 1, lon), device_id_type=MESH)
-
-    @pl.when(has_south)
-    def _():
-        pl.semaphore_signal(barrier, inc=1, device_id=(lat + 1, lon), device_id_type=MESH)
+
+    def greet(j, _):
+        pl.semaphore_signal(barrier, inc=1, device_id=place_of(j)[1], device_id_type=MESH)
+        return 0
+
+    lax.fori_loop(1, total_count, greet, 0)
+    pl.semaphore_wait(barrier, total_count - 1)
+
+    def send(j, _):
+        other, place = place_of(j)
+        pltpu.make_async_remote_copy(
+            src_ref=packed_ref.at[other], dst_ref=got_ref.at[me],
+            send_sem=out_sem.at[other], recv_sem=in_sem.at[me],
+            device_id=place, device_id_type=MESH,
+        ).start()
+        return 0
+
+    lax.fori_loop(1, total_count, send, 0)
+    got_ref[me] = packed_ref[me]
 
     @pl.when(jnp.logical_not(has_north))
     def _():
@@ -133,6 +152,43 @@
     @pl.when(jnp.logical_not(has_south))
     def _():
         row_in[:, 1] = jnp.zeros((steps, tracers, layers, cols), F32)
+
+    den = 1.0 + mixing_ref[0]
+    inv = 1.0 / den
+    inverse[0] = inv
+    upper[0] = -mixing_ref[0] * inv
+
+    def setup(k, up):
+        low = mixing_ref[k - 1]
+        high = mixing_ref[k]
+        inv = 1.0 / ((1.0 + low + high) + low * up)
+        inverse[k] = inv
+        up = -high * inv
+        upper[k] = up
+        return up
+
+    up = lax.fori_loop(1, layers - 1, setup, upper[0])
+    low = mixing_ref[layers - 2]
+    inverse[layers - 1] = 1.0 / ((1.0 + low) + low * up)
+
+    def middle(k, _):
+        center[k] = (
+            1.0 - transport_ref[0, k] - transport_ref[1, k] - transport_ref[2, k] - transport_ref[3, k]
+        )
+        return 0
+
+    lax.fori_loop(0, layers, middle, 0)
+
+    def settle(j, _):
+        other, place = place_of(j)
+        pltpu.make_async_remote_copy(
+            src_ref=packed_ref.at[other], dst_ref=got_ref.at[other],
+            send_sem=out_sem.at[other], recv_sem=in_sem.at[other],
+            device_id=place, device_id_type=MESH,
+        ).wait()
+        return 0
+
+    lax.fori_loop(1, total_count, settle, 0)
 
     per = got_ref.shape[0] * 128 // slot_count
     cap = 128 // per
@@ -148,32 +204,6 @@
                 here = (slot_lane >= member * cap) & (slot_lane < (member + 1) * cap)
                 total = jnp.where(here, block, total)
             slots[step * FIELDS : (step + 1) * FIELDS, group * 128 : (group + 1) * 128] = total
-
-    den = 1.0 + mixing_ref[0]
-    inv = 1.0 / den
-    inverse[0] = inv
-    upper[0] = -mixing_ref[0] * inv
-
-    def setup(k, up):
-        low = mixing_ref[k - 1]
-        high = mixing_ref[k]
-        inv = 1.0 / ((1.0 + low + high) + low * up)
-        inverse[k] = inv
-        up = -high * inv
-        upper[k] = up
-        return up
-
-    up = lax.fori_loop(1, layers - 1, setup, upper[0])
-    low = mixing_ref[layers - 2]
-    inverse[layers - 1] = 1.0 / ((1.0 + low) + low * up)
-
-    def middle(k, _):
-        center[k] = (
-            1.0 - transport_ref[0, k] - transport_ref[1, k] - transport_ref[2, k] - transport_ref[3, k]
-        )
-        return 0
-
-    lax.fori_loop(0, layers, middle, 0)
 
     table_parts = [part.astype(BF16) for part in parts(table_ref[...], 3)]
     channel = layers * half
@@ -331,9 +361,6 @@
 
         lax.fori_loop(1, layers, level, 0, unroll=5)
 
-    count = 2 + has_north.astype(jnp.int32) + has_south.astype(jnp.int32)
-    pl.semaphore_wait(barrier, count)
-
     observe(steps - 1)
     for step in range(steps - 1, -1, -1):
         sweep_up(step)
@@ -395,7 +422,6 @@
         out_specs=vmem,
         compiler_params=pltpu.CompilerParams(vmem_limit_bytes=40 << 20),
     )(track_tile[:, :, 0], sound_cell, kernel_index, observed, precision)
-    got = lax.all_to_all(packed, ("lat", "lon"), split_axis=0, concat_axis=0, tiled=True)
     slot_count = tile_count * cap
     field = (tracers, layers, rows, cols)
     return pl.pallas_call(
@@ -404,6 +430,7 @@
         in_specs=[vmem] * 5,
         out_specs=(vmem, vmem),
         scratch_shapes=[
+            pltpu.VMEM((tile_count, FIELDS, 128), F32),
             pltpu.VMEM((steps * FIELDS, slot_count), F32),
             pltpu.VMEM((layers, slot_count), F32),
             pltpu.VMEM((tracers, 2, layers, slot_count), F32),
@@ -421,11 +448,13 @@
             pltpu.VMEM((tracers, rows, cols), F32),
             pltpu.SemaphoreType.DMA((steps, 4)),
             pltpu.SemaphoreType.DMA((steps, 4)),
+            pltpu.SemaphoreType.DMA((tile_count,)),
+            pltpu.SemaphoreType.DMA((tile_count,)),
         ],
         compiler_params=pltpu.CompilerParams(
             collective_id=0, has_side_effects=True, vmem_limit_bytes=48 << 20
         ),
-    )(got, kernel_table.T, transport, mixing, trajectory)
+    )(packed, kernel_table.T, transport, mixing, trajectory)
 
 
 def solution(mesh):

time: 66.6 us -> 62.3 us (0.935)
  blocking collectives: 14.8 us -> 0 us
  Pallas kernels: 41.7 us -> 52.3 us
    all_to_all x1 -> x0, blocking collectives: 14.8 us -> none  [body(): lax.all_to_all(packed, ('lat', 'lon'), split_axis=0, concat_axis=0, tiled...]
    pallas_call x1, Pallas kernels: 40.1 us -> 50.6 us  [body(): pl.pallas_call(functools.partial(window_kernel, lat_count, lon_count), ou...]
where the time goes in v3:
time: 62.3 us; the launch traced here: 61.8 us
  Pallas kernels  52.3 us (84%)
  local copies, waits for them, and re-layouts  8.81 us (14%)
  between operations  0.67 us (1%)
    pallas_call x1, Pallas kernels, body(): pl.pallas_call(functools.partial(window_kernel, lat_count, lon_count), ou...  50.6 us
    unnamed x16, local copies, waits for them, and re-layouts  8.81 us
    pallas_call x1, Pallas kernels, body(): pl.pallas_call(functools.partial(pack_kernel, cap, rows // 2, cols), out_...  1.63 us

profile of v3, /device:TPU:0, one launch (start us, length us, event | category | flops | bytes accessed | tf_op | source)
XLA Modules:
  0.0 61.8 jit_solution(13051733684398200260)
XLA Ops:
  0.6 0.7 %copy.14 = s32[4,512,1]{1,0,2:T(4,128)S(1)} copy(s32[4,512,1]{1,2,0:T(1,128)} %param.13) | data formatting | bytes 16384
  1.3 0.8 %copy.11.obs_ref = f32[4,3,512]{2,1,0:T(4,128)S(1)} copy(f32[4,3,512]{2,0,1:T(4,128)} %param.16) | data formatting | bytes 49152 | tf_op args[7]
  2.1 0.0 copy-start.3
  2.1 0.7 %copy-done.3 = s32[4,512]{1,0:T(4,128)S(1)} copy-done((s32[4,512]{1,0:T(4,128)S(1)}, s32[4,512]{1,0:T(4,128)}, u32[]{:S(2)}) %copy-start.3) | copy-done | bytes 8216
  2.8 0.0 copy-start.4
  2.8 0.7 %copy-done.4 = s32[4,512]{1,0:T(4,128)S(1)} copy-done((s32[4,512]{1,0:T(4,128)S(1)}, s32[4,512]{1,0:T(4,128)}, u32[]{:S(2)}) %copy-start.4) | copy-done | bytes 8216
  3.5 0.0 copy-start.5
  3.5 0.7 %copy-done.5 = f32[4,512]{1,0:T(4,128)S(1)} copy-done((f32[4,512]{1,0:T(4,128)S(1)}, f32[4,512]{1,0:T(4,128)}, u32[]{:S(2)}) %copy-start.5) | copy-done | bytes 8216
  4.2 1.6 %shard_map.104.packed_ref = f32[32,8,128]{2,1,0:T(8,128)S(1)} custom-call(s32[4,512]{1,0:T(4,128)S(1)} %bitcast.4, s32[4,512]{1,0:T(4,128)S(1)} %copy-done.3, s32[4,512]{1,0:T(4,128)S(1)} %copy-done.4, f32[4,3,512]{2,1,0:T(4,128)S(1)} %copy.11.obs_ref, f32[4,512]{1,0:T(4,128)S(1)} %copy-done.5), custom_call_target="tpu_custom_call" | custom-call | tf_op jit(solution)/shard_map/pallas_call | solution.py:418
  5.8 0.0 copy-start
  5.8 1.7 %copy-done = f32[4,36,32,128]{3,2,1,0:T(8,128)S(1)} copy-done((f32[4,36,32,128]{3,2,1,0:T(8,128)S(1)}, f32[4,36,32,128]{3,2,1,0:T(8,128)}, u32[]{:S(2)}) %copy-start) | copy-done | bytes 2359320
  7.5 0.0 copy-start.1
  7.5 1.1 %copy-done.1 = f32[35,32,128]{2,1,0:T(8,128)S(1)} copy-done((f32[35,32,128]{2,1,0:T(8,128)S(1)}, f32[35,32,128]{2,1,0:T(8,128)}, u32[]{:S(2)}) %copy-start.1) | copy-done | bytes 573464
  8.5 0.0 copy-start.2
  8.5 0.7 %copy-done.2 = f32[64,36]{0,1:T(8,128)S(1)} copy-done((f32[64,36]{0,1:T(8,128)S(1)}, f32[64,36]{0,1:T(8,128)}, u32[]{:S(2)}) %copy-start.2) | copy-done | bytes 9240
  9.3 50.6 %shard_map.105 = (f32[3,36,32,128]{3,2,1,0:T(8,128)S(1)}, f32[3,32,128]{2,1,0:T(8,128)S(1)}) custom-call(f32[32,8,128]{2,1,0:T(8,128)S(1)} %shard_map.104.packed_ref, f32[36,64]{1,0:T(8,128)S(1)} %bitcast.5, f32[4,36,32,128]{3,2,1,0:T(8,128)S(1)} %copy-done, f32[35,32,128]{2,1,0:T(8,128)S(1)} %copy-done.1, bf16[4,3,36,32,128]{4,3,2,1,0:T(8,128)(2,1)} %trajectory_ref.1), custom_call_target="tpu_custom_call" | custom-call | tf_op jit(solution)/shard_map/pallas_call | solution.py:427
  59.9 1.2 %copy.17 = f32[3,36,32,128]{3,2,1,0:T(8,128)} copy(f32[3,36,32,128]{3,2,1,0:T(8,128)S(1)} %get-tuple-element.4) | data formatting | bytes 3538944
  61.1 0.6 %copy.18 = f32[3,32,128]{2,1,0:T(8,128)} copy(f32[3,32,128]{2,1,0:T(8,128)S(1)} %get-tuple-element.5) | data formatting | bytes 98304
Async XLA Ops:
  2.1 0.7 %copy-start.3 = (s32[4,512]{1,0:T(4,128)S(1)}, s32[4,512]{1,0:T(4,128)}, u32[]{:S(2)}) copy-start(s32[4,512]{1,0:T(4,128)} %cell_ref.1) | copy-start | bytes 24580
  2.8 0.7 %copy-start.4 = (s32[4,512]{1,0:T(4,128)S(1)}, s32[4,512]{1,0:T(4,128)}, u32[]{:S(2)}) copy-start(s32[4,512]{1,0:T(4,128)} %index_ref.1) | copy-start | bytes 24580
  3.5 0.7 %copy-start.5 = (f32[4,512]{1,0:T(4,128)S(1)}, f32[4,512]{1,0:T(4,128)}, u32[]{:S(2)}) copy-start(f32[4,512]{1,0:T(4,128)} %prec_ref.1) | copy-start | bytes 24580
  5.8 1.7 %copy-start = (f32[4,36,32,128]{3,2,1,0:T(8,128)S(1)}, f32[4,36,32,128]{3,2,1,0:T(8,128)}, u32[]{:S(2)}) copy-start(f32[4,36,32,128]{3,2,1,0:T(8,128)} %transport_ref.1) | copy-start | bytes 7077892
  7.5 1.1 %copy-start.1 = (f32[35,32,128]{2,1,0:T(8,128)S(1)}, f32[35,32,128]{2,1,0:T(8,128)}, u32[]{:S(2)}) copy-start(f32[35,32,128]{2,1,0:T(8,128)} %mixing_ref.1) | copy-start | bytes 1720324
  8.5 0.7 %copy-start.2 = (f32[64,36]{0,1:T(8,128)S(1)}, f32[64,36]{0,1:T(8,128)}, u32[]{:S(2)}) copy-start(f32[64,36]{0,1:T(8,128)} %param.12) | copy-start | bytes 27652
